TPU v7x, 32 devices: a whole 2x2x4 slice. The times are simulated.
32 devices in a mesh: dp: 16 (over z, y, x), tensor: 2 (over core).
Axes of the slice: x: 2, y: 2, z: 4, core: 2. Of those that a mesh axis runs over, the one named last changes fastest.
Arguments:
- layer_in: bfloat16 [32, 584, 1024], P('dp', 'tensor'), may hold values from -6 to 6
- out_grad: bfloat16 [32, 584, 1024], P('dp', 'tensor'), may hold values from -6 to 6
- key_valid: int32 [32, 584], P('dp'), may hold values from 0 to 1, as said below
- image_live: int32 [32], P('dp'), may hold values 0 or 1
- w_qkv: bfloat16 [3, 1024, 1024], P(None, 'dp', 'tensor'), may hold values from -0.1875 to 0.1875
- w_out: bfloat16 [1024, 1024], P('tensor', 'dp'), may hold values from -2 to 2
- w_fc1: bfloat16 [1024, 4096], P('dp', 'tensor'), may hold values from -0.1875 to 0.1875
- w_fc2: bfloat16 [4096, 1024], P('tensor', 'dp'), may hold values from -0.09375 to 0.09375
- norm_gains: bfloat16 [2, 1024], P(None, 'dp'), may hold values from 0.5 to 1.5
- bias_rows: bfloat16 [6, 1024], P(None, 'dp'), may hold values from -1.1953125 to 1.1953125
- fc_bias: bfloat16 [4096], P('dp'), may hold values from -1.796875 to 1.796875
Outputs:
- layer_out: bfloat16 [32, 584, 1024], P('dp', 'tensor')
- input_grad: bfloat16 [32, 584, 1024], P('dp', 'tensor')
- grad_w_qkv: float32 [3, 1024, 1024], P(None, 'dp', 'tensor')
- grad_w_out: float32 [1024, 1024], P('tensor', 'dp')
- grad_w_fc1: float32 [1024, 4096], P('dp', 'tensor')
- grad_w_fc2: float32 [4096, 1024], P('tensor', 'dp')
- grad_vectors: float32 [8, 1024], P(None, ('dp', 'tensor'))
- grad_fc_bias: float32 [4096], P(('dp', 'tensor'))
Inputs may be any that keep to these rules, and one draw needn't show every extreme that they name: `key_valid`: key 0 of every image is 1, and every key at a position of 577 or more is 0.
All inputs are finite; a program needn't handle non-finite values. No bound on the sum of `image_live` on one device may be relied on, other than what follows from the above.
Results may differ from a plain program's by a relative error of at most 0.015.
Values may be sent and summed in bfloat16 or wider, within the bound.
A program may use at most 256 MiB of HBM per device.

v0:
```python
import jax
import jax.numpy as jnp
from jax import lax
from jax.sharding import PartitionSpec as P

D = 1024
HEAD_DIM = 64
FF = 4096
MICRO = 2
IMG_MB = 1


EPSILON = 1e-05


def norm_forward(values, gain_row, shift_row):
    centred = values - jnp.mean(values, axis=-1, keepdims=True)
    inverse = lax.rsqrt(jnp.mean(centred * centred, axis=-1, keepdims=True) + EPSILON)
    normed = centred * inverse
    return (normed * gain_row + shift_row, normed, inverse)


def norm_backward(upstream, normed, inverse, gain_row):
    scaled = upstream * gain_row
    return inverse * (
        scaled
        - jnp.mean(scaled, axis=-1, keepdims=True)
        - normed * jnp.mean(scaled * normed, axis=-1, keepdims=True)
    )


def pair_slice(source, pair_index):
    pair_width = 2 * HEAD_DIM
    sliced = lax.dynamic_slice_in_dim(source, pair_index * pair_width, pair_width, 2)
    return sliced.reshape(sliced.shape[0], sliced.shape[1], 2, HEAD_DIM)


def pair_scores(query_block, key_block, valid_keys, score_scale):
    scores = (
        jnp.einsum("bqhd,bkhd->bhqk", query_block, key_block, preferred_element_type=jnp.float32)
        * score_scale
    )
    return jnp.where(valid_keys[:, None, None, :], scores, -1000000000.0)


def join_pairs(stacked):
    pair_count, batch_size, seq_length, pair_width = stacked.shape
    return jnp.transpose(stacked, (1, 2, 0, 3)).reshape(
        batch_size, seq_length, pair_count * pair_width
    )


def attend_forward(queries, key_rows, value_rows, valid_keys, score_scale):
    batch_size, seq_length, local_cols = queries.shape
    pair_count = local_cols // (2 * HEAD_DIM)

    def one_pair(pair_index):
        scores = pair_scores(
            pair_slice(queries, pair_index),
            pair_slice(key_rows, pair_index),
            valid_keys,
            score_scale,
        )
        row_max = jnp.max(scores, axis=-1, keepdims=True)
        expons = jnp.exp(scores - row_max)
        row_total = jnp.sum(expons, axis=-1, keepdims=True)
        attn_probs = (expons / row_total).astype(jnp.bfloat16)
        mixed_rows = jnp.einsum(
            "bhqk,bkhd->bqhd",
            attn_probs,
            pair_slice(value_rows, pair_index),
            preferred_element_type=jnp.float32,
        )
        mixed_rows = mixed_rows.reshape(batch_size, seq_length, 2 * HEAD_DIM).astype(jnp.bfloat16)
        return (mixed_rows, (row_max + jnp.log(row_total))[..., 0])

    blocks, log_totals = lax.map(one_pair, jnp.arange(pair_count))
    return (join_pairs(blocks), log_totals)


def attend_backward(
    queries, key_rows, value_rows, attended_grad, log_totals, valid_keys, score_scale
):
    batch_size, seq_length, local_cols = queries.shape
    pair_count = local_cols // (2 * HEAD_DIM)

    def one_pair(inputs):
        pair_index, pair_totals = inputs
        query_block = pair_slice(queries, pair_index)
        key_block = pair_slice(key_rows, pair_index)
        value_block = pair_slice(value_rows, pair_index)
        grad_block = pair_slice(attended_grad, pair_index)
        scores = pair_scores(query_block, key_block, valid_keys, score_scale)
        attn_probs = jnp.exp(scores - pair_totals[..., None])
        prob_grad = jnp.einsum(
            "bqhd,bkhd->bhqk", grad_block, value_block, preferred_element_type=jnp.float32
        )
        centre = jnp.sum(attn_probs * prob_grad, axis=-1, keepdims=True)
        score_grad = (attn_probs * (prob_grad - centre) * score_scale).astype(jnp.bfloat16)
        query_grad = jnp.einsum(
            "bhqk,bkhd->bqhd", score_grad, key_block, preferred_element_type=jnp.float32
        )
        key_grad = jnp.einsum(
            "bhqk,bqhd->bkhd", score_grad, query_block, preferred_element_type=jnp.float32
        )
        value_grad = jnp.einsum(
            "bhqk,bqhd->bkhd",
            attn_probs.astype(jnp.bfloat16),
            grad_block,
            preferred_element_type=jnp.float32,
        )
        return tuple(
            (
                member.reshape(batch_size, seq_length, 2 * HEAD_DIM).astype(jnp.bfloat16)
                for member in (query_grad, key_grad, value_grad)
            )
        )

    grad_parts = lax.map(one_pair, (jnp.arange(pair_count), log_totals))
    return tuple((join_pairs(member) for member in grad_parts))


def shards(
    layer_in,
    out_grad,
    key_valid,
    image_live,
    w_qkv,
    w_out,
    w_fc1,
    w_fc2,
    norm_gains,
    bias_rows,
    fc_bias,
):
    tensor_index = lax.axis_index("tensor")
    local_width = w_qkv.shape[2]
    hidden_local = w_fc1.shape[1]
    score_scale = HEAD_DIM ** (-0.5)
    outputs = []
    input_grads = []
    weight_totals = None
    vector_total = jnp.zeros((8, D), jnp.float32)
    fc_total = jnp.zeros((FF,), jnp.float32)
    zero_row = jnp.zeros((D,), jnp.float32)
    zero_hidden = jnp.zeros((FF,), jnp.float32)
    for micro_step in range(MICRO):
        first_img = micro_step * IMG_MB
        tokens = layer_in[first_img : first_img + IMG_MB].astype(jnp.float32)
        live_rows = image_live[first_img : first_img + IMG_MB].astype(jnp.float32)[:, None, None]
        grad_local = out_grad[first_img : first_img + IMG_MB].astype(jnp.float32) * live_rows
        grad_low = grad_local.astype(jnp.bfloat16)
        valid_keys = key_valid[first_img : first_img + IMG_MB] > 0
        gathered = (
            lax.all_gather(w_qkv, "dp", axis=1, tiled=True),
            lax.all_gather(w_out, "dp", axis=1, tiled=True),
            lax.all_gather(w_fc1, "dp", axis=0, tiled=True),
            lax.all_gather(w_fc2, "dp", axis=1, tiled=True),
            lax.all_gather(norm_gains, "dp", axis=1, tiled=True),
            lax.all_gather(bias_rows, "dp", axis=1, tiled=True),
            lax.all_gather(fc_bias, "dp", axis=0, tiled=True),
        )
        qkv_weight, out_weight, up_weight, down_weight, gain_rows, shift_rows, hidden_shift = (
            gathered
        )
        gain_rows = gain_rows.astype(jnp.float32)
        shift_rows = shift_rows.astype(jnp.float32)
        query_bias = lax.dynamic_slice_in_dim(
            shift_rows[1], tensor_index * local_width, local_width
        )
        value_bias = lax.dynamic_slice_in_dim(
            shift_rows[2], tensor_index * local_width, local_width
        )
        hidden_bias = lax.dynamic_slice_in_dim(
            hidden_shift.astype(jnp.float32), tensor_index * hidden_local, hidden_local
        )
        first, first_normed, first_inverse = norm_forward(tokens, gain_rows[0], shift_rows[0])
        first_full = lax.all_gather(first.astype(jnp.bfloat16), "tensor", axis=1, tiled=True)
        projected = jnp.einsum(
            "bsd,cde->cbse", first_full, qkv_weight, preferred_element_type=jnp.float32
        )
        queries = (projected[0] + query_bias).astype(jnp.bfloat16)
        key_rows = projected[1].astype(jnp.bfloat16)
        value_rows = (projected[2] + value_bias).astype(jnp.bfloat16)
        attended, log_totals = attend_forward(
            queries, key_rows, value_rows, valid_keys, score_scale
        )
        attn_terms = jnp.einsum(
            "bsl,ld->bsd", attended, out_weight, preferred_element_type=jnp.float32
        )
        middle = (
            tokens
            + lax.psum_scatter(
                attn_terms.astype(jnp.bfloat16), "tensor", scatter_dimension=1, tiled=True
            ).astype(jnp.float32)
            + shift_rows[3]
        )
        second, second_normed, second_inverse = norm_forward(middle, gain_rows[1], shift_rows[4])
        second_full = lax.all_gather(second.astype(jnp.bfloat16), "tensor", axis=1, tiled=True)
        hidden = (
            jnp.einsum("bsd,df->bsf", second_full, up_weight, preferred_element_type=jnp.float32)
            + hidden_bias
        )
        gate_sig = jax.nn.sigmoid(1.702 * hidden)
        activated = (hidden * gate_sig).astype(jnp.bfloat16)
        mlp_terms = jnp.einsum(
            "bsf,fd->bsd", activated, down_weight, preferred_element_type=jnp.float32
        )
        layer_rows = (
            middle
            + lax.psum_scatter(
                mlp_terms.astype(jnp.bfloat16), "tensor", scatter_dimension=1, tiled=True
            ).astype(jnp.float32)
            + shift_rows[5]
        )
        outputs.append(layer_rows.astype(jnp.bfloat16))
        grad_full = lax.all_gather(grad_low, "tensor", axis=1, tiled=True)
        down_grad = jnp.einsum(
            "bsf,bsd->fd", activated, grad_full, preferred_element_type=jnp.float32
        )
        act_grad = jnp.einsum(
            "bsd,fd->bsf", grad_full, down_weight, preferred_element_type=jnp.float32
        )
        hidden_grad = (act_grad * (gate_sig + 1.702 * hidden * gate_sig * (1.0 - gate_sig))).astype(
            jnp.bfloat16
        )
        up_grad = jnp.einsum(
            "bsd,bsf->df", second_full, hidden_grad, preferred_element_type=jnp.float32
        )
        second_terms = jnp.einsum(
            "bsf,df->bsd", hidden_grad, up_weight, preferred_element_type=jnp.float32
        )
        second_grad = lax.psum_scatter(
            second_terms.astype(jnp.bfloat16), "tensor", scatter_dimension=1, tiled=True
        ).astype(jnp.float32)
        middle_grad = grad_local + norm_backward(
            second_grad, second_normed, second_inverse, gain_rows[1]
        )
        middle_low = middle_grad.astype(jnp.bfloat16)
        middle_full = lax.all_gather(middle_low, "tensor", axis=1, tiled=True)
        out_w_grad = jnp.einsum(
            "bsl,bsd->ld", attended, middle_full, preferred_element_type=jnp.float32
        )
        attended_grad = jnp.einsum(
            "bsd,ld->bsl", middle_full, out_weight, preferred_element_type=jnp.float32
        ).astype(jnp.bfloat16)
        query_grad, key_grad, value_grad = attend_backward(
            queries, key_rows, value_rows, attended_grad, log_totals, valid_keys, score_scale
        )
        stacked_grad = jnp.stack([query_grad, key_grad, value_grad])
        qkv_grad = jnp.einsum(
            "bsd,cbse->cde", first_full, stacked_grad, preferred_element_type=jnp.float32
        )
        first_terms = jnp.einsum(
            "cbse,cde->bsd", stacked_grad, qkv_weight, preferred_element_type=jnp.float32
        )
        first_grad = lax.psum_scatter(
            first_terms.astype(jnp.bfloat16), "tensor", scatter_dimension=1, tiled=True
        ).astype(jnp.float32)
        input_rows = middle_grad + norm_backward(
            first_grad, first_normed, first_inverse, gain_rows[0]
        )
        input_grads.append(input_rows.astype(jnp.bfloat16))
        micro_vectors = jnp.stack(
            [
                jnp.sum(first_grad * first_normed, axis=(0, 1)),
                jnp.sum(first_grad, axis=(0, 1)),
                lax.dynamic_update_slice_in_dim(
                    zero_row,
                    jnp.sum(query_grad, axis=(0, 1), dtype=jnp.float32),
                    tensor_index * local_width,
                    0,
                ),
                lax.dynamic_update_slice_in_dim(
                    zero_row,
                    jnp.sum(value_grad, axis=(0, 1), dtype=jnp.float32),
                    tensor_index * local_width,
                    0,
                ),
                jnp.sum(middle_low, axis=(0, 1), dtype=jnp.float32),
                jnp.sum(second_grad * second_normed, axis=(0, 1)),
                jnp.sum(second_grad, axis=(0, 1)),
                jnp.sum(grad_local, axis=(0, 1)),
            ]
        )
        vector_total = vector_total + micro_vectors
        fc_total = fc_total + lax.dynamic_update_slice_in_dim(
            zero_hidden,
            jnp.sum(hidden_grad, axis=(0, 1), dtype=jnp.float32),
            tensor_index * hidden_local,
            0,
        )
        micro_grads = (qkv_grad, out_w_grad, up_grad, down_grad)
        if weight_totals is None:
            weight_totals = micro_grads
        else:
            weight_totals = tuple(
                (before + added for before, added in zip(weight_totals, micro_grads))
            )
    weight_totals = (
        lax.psum_scatter(weight_totals[0], "dp", scatter_dimension=1, tiled=True),
        lax.psum_scatter(weight_totals[1], "dp", scatter_dimension=1, tiled=True),
        lax.psum_scatter(weight_totals[2], "dp", scatter_dimension=0, tiled=True),
        lax.psum_scatter(weight_totals[3], "dp", scatter_dimension=1, tiled=True),
    )
    summed_vectors, summed_hidden = (
        lax.psum_scatter(vector_total, ("dp", "tensor"), scatter_dimension=1, tiled=True),
        lax.psum_scatter(fc_total, ("dp", "tensor"), scatter_dimension=0, tiled=True),
    )
    return (
        jnp.concatenate(outputs, axis=0),
        jnp.concatenate(input_grads, axis=0),
        weight_totals[0],
        weight_totals[1],
        weight_totals[2],
        weight_totals[3],
        summed_vectors,
        summed_hidden,
    )


def solution(mesh):
    return jax.shard_map(
        shards,
        mesh=mesh,
        in_specs=(
            P("dp", "tensor", None),
            P("dp", "tensor", None),
            P("dp", None),
            P("dp"),
            P(None, "dp", "tensor"),
            P("tensor", "dp"),
            P("dp", "tensor"),
            P("tensor", "dp"),
            P(None, "dp"),
            P(None, "dp"),
            P("dp"),
        ),
        out_specs=(
            P("dp", "tensor", None),
            P("dp", "tensor", None),
            P(None, "dp", "tensor"),
            P("tensor", "dp"),
            P("dp", "tensor"),
            P("tensor", "dp"),
            P(None, ("dp", "tensor")),
            P(("dp", "tensor")),
        ),
        check_vma=False,
    )
```

profile of v0, /device:TPU:0, one launch (start us, length us, event | category | flops | bytes accessed | tf_op | source)
XLA Modules:
  0.0 1656.5 jit_solution(3379858513073067699)
XLA Ops:
  7.2 5.1 convert_reduce_fusion.9
  12.4 8.2 multiply_reduce_fusion.13
  20.6 42.2 %all-gather = bf16[16,64,2]{1,2,0:T(2,128)(2,1)S(1)} all-gather(bf16[1,64,2]{1,2,0:T(2,128)(2,1)S(1)} %bitcast.546), channel_id=1, replica_groups=mesh['dp'=16,'tensor'=2] {'dp'}, dimensions={0}, use_global_device_ids=true | all-gather | bytes 4352 | tf_op jit(solution)/shard_map/all_gather | solution.py:159
  62.9 35.6 %all-gather.1 = bf16[16,64,6]{1,2,0:T(8,128)(2,1)S(1)} all-gather(bf16[1,64,6]{1,2,0:T(8,128)(2,1)S(1)} %bitcast.545), channel_id=1, replica_groups=mesh['dp'=16,'tensor'=2] {'dp'}, dimensions={0}, use_global_device_ids=true | all-gather | bytes 13056 | tf_op jit(solution)/shard_map/all_gather | solution.py:160
  99.2 6.2 add_convert_fusion.5
  107.7 6.6 all-gather.28.cloned.1.call-done
  114.3 71.6 %all-gather.18.cloned.1.call-done = bf16[3,1024,512]{2,1,0:T(8,128)(2,1)} async-done(((bf16[3,64,512]{2,1,0:T(8,128)(2,1)}), bf16[3,1024,512]{2,1,0:T(8,128)(2,1)}) %all-gather.18.cloned.1.call-update) | async-done | bytes 3145744 | tf_op jit(solution)/shard_map/all_gather | solution.py:155
  185.9 4.6 convolution_bitcast_fusion
  193.5 4.7 all-gather.16.cloned.1.call-done
  198.2 4.8 fusion.113
  210.9 23.2 %while.53 = (s32[]{:T(128)}, bf16[4,1,584,128]{2,3,1,0:T(8,128)(2,1)S(1)}, f32[4,1,2,584]{3,2,1,0:T(2,128)S(1)}, s32[4]{0:T(128)S(1)}, bf16[1,584,512]{1,2,0:T(8...) while((s32[]{:T(128)}, ...), condition=%wide.region_15.16_spmd, body=%wide.region_12.15_spmd.sunk | while | flops 182879600 | bytes 10049912 | solution.py:77
  236.4 23.2 %while.52 = (s32[]{:T(128)}, bf16[4,1,584,128]{2,3,1,0:T(8,128)(2,1)S(1)}, f32[4,1,2,584]{3,2,1,0:T(2,128)S(1)}, s32[4]{0:T(128)S(1)}, bf16[1,584,512]{1,2,0:T(8...) while((s32[]{:T(128)}, ...), condition=%wide.region_5.6_spmd, body=%wide.region_2.5_spmd.sunk | while | flops 182879600 | bytes 10049912 | solution.py:77
  265.0 6.4 fusion.167
  279.4 5.6 fusion.168
  292.3 5.2 add_convert_fusion.4
  305.5 41.4 %all-gather.2 = bf16[16,1,256]{2,1,0:T(2,128)(2,1)S(1)} all-gather(bf16[1,1,256]{2,1,0:T(2,128)(2,1)S(1)} %reshape.955), channel_id=1, replica_groups=mesh['dp'=16,'tensor'=2] {'dp'}, dimensions={0}, use_global_device_ids=true | all-gather | bytes 8704 | tf_op jit(solution)/shard_map/all_gather | solution.py:161
  347.0 42.6 %all-gather.24.cloned.1.call-done = bf16[1024,2048]{1,0:T(8,128)(2,1)} async-done(((bf16[64,2048]{1,0:T(8,128)(2,1)}), bf16[1024,2048]{1,0:T(8,128)(2,1)}) %all-gather.24.cloned.1.call-update) | async-done | bytes 4194320 | tf_op jit(solution)/shard_map/all_gather | solution.py:157
  389.6 7.8 fusion.95
  400.7 80.1 %all-gather.26.cloned.1.call-done = bf16[2048,1024]{0,1:T(8,128)(2,1)} async-done(((bf16[2048,64]{0,1:T(8,128)(2,1)}), bf16[2048,1024]{0,1:T(8,128)(2,1)}) %all-gather.26.cloned.1.call-update) | async-done | bytes 4194320 | tf_op jit(solution)/shard_map/all_gather | solution.py:158
  480.8 10.2 convert_reduce_fusion
  492.6 7.9 fusion.106
  500.4 3.7 fusion.81
  506.2 9.1 convert_reduce_fusion.1
  516.8 3.7 fusion.80
  520.5 6.8 fusion.166
  531.4 4.9 concatenate.12
  537.6 4.9 concatenate.14
  543.7 11.8 multiply_reduce_fusion.4
  555.5 13.0 fusion.163
  571.5 7.5 fusion.79
  579.0 6.9 fusion.78
  594.1 73.7 %while.55 = (s32[]{:T(128)}, bf16[4,1,584,128]{2,3,1,0:T(8,128)(2,1)}, bf16[4,1,584,128]{2,3,1,0:T(8,128)(2,1)}, bf16[4,1,584,128]{2,3,1,0:T(8,128)(2,1)}, s32[4...) while((s32[]{:T(128)}, ...), condition=%wide.region_34.35_spmd, body=%wide.region_32.34_spmd.sunk | while | flops 446329024 | bytes 23643488 | solution.py:119
  602.5 4.3 fusion.302
  620.9 4.3 fusion.302
  639.3 4.3 fusion.302
  657.7 4.3 fusion.302
  679.7 74.0 %while.54 = (s32[]{:T(128)}, bf16[4,1,584,128]{2,3,1,0:T(8,128)(2,1)}, bf16[4,1,584,128]{2,3,1,0:T(8,128)(2,1)}, bf16[4,1,584,128]{2,3,1,0:T(8,128)(2,1)}, s32[4...) while((s32[]{:T(128)}, ...), condition=%wide.region_25.26_spmd, body=%wide.region_23.25_spmd.sunk | while | flops 446329024 | bytes 23643304 | solution.py:119
  688.1 4.3 fusion.288
  706.5 4.3 fusion.288
  724.9 4.3 fusion.288
  743.3 4.3 fusion.288
  758.9 5.2 fusion.77
  767.3 9.3 fusion.165
  780.1 7.5 fusion.111
  787.6 4.2 concatenate.13
  793.2 4.9 concatenate.15
  799.4 11.2 multiply_reduce_fusion.5
  812.1 9.6 add_bitcast_fusion
  821.7 9.4 copy.214
  838.1 6.5 fusion.108
  844.6 8.7 convolution_add_fusion
  853.4 6.2 fusion.104
  859.6 6.1 convolution_add_fusion.1
  871.3 41.1 %all-reduce.9 = f32[4096]{0:T(1024)S(1)} all-reduce(f32[4096]{0:T(1024)S(1)} %add_dynamic-update-slice_fusion), channel_id=15, replica_groups=mesh['dp'=16,'tensor'=2] {'dp','tensor'}, use_global_device_ids=true, to_apply=%region_61.62.clone | all-reduce | flops 4096 | bytes 32768
  913.0 4.2 concatenate.9
  917.2 5.0 concatenate.11
  927.4 3.7 pad_maximum_fusion
  931.2 7.5 add_convert_fusion.1
  938.8 3.7 pad_maximum_fusion.1
  942.5 4.7 reduce-scatter.37.cloned.1.call-done
  948.6 257.9 %all-reduce.23.cloned.1.call-done = f32[3,1024,512]{2,0,1:T(4,128)} async-done(((f32[3,1024,512]{2,0,1:T(4,128)}), f32[3,1024,512]{2,0,1:T(4,128)}) %all-reduce.23.cloned.1.call-update) | async-done | bytes 6291472
  1208.4 80.3 %reduce-scatter.31.cloned.1.call-done = f32[512,64]{0,1:T(8,128)} async-done(((f32[512,1024]{0,1:T(8,128)}), f32[512,64]{0,1:T(8,128)}) %reduce-scatter.31.cloned.1.call-update) | async-done | bytes 131088 | tf_op jit(solution)/shard_map/reduce_scatter | solution.py:302
  1288.7 177.9 %reduce-scatter.35.cloned.1.call-done = f32[2048,64]{0,1:T(8,128)} async-done(((f32[2048,1024]{0,1:T(8,128)}), f32[2048,64]{0,1:T(8,128)}) %reduce-scatter.35.cloned.1.call-update) | async-done | bytes 524304 | tf_op jit(solution)/shard_map/reduce_scatter | solution.py:304
  1466.6 183.1 %reduce-scatter.33.cloned.1.call-done = f32[64,2048]{1,0:T(8,128)} async-done(((f32[1024,2048]{1,0:T(8,128)}), f32[64,2048]{1,0:T(8,128)}) %reduce-scatter.33.cloned.1.call-update) | async-done | bytes 524304 | tf_op jit(solution)/shard_map/reduce_scatter | solution.py:303
  (535 shorter events, 265.1 us)
Async XLA Ops:
  7.2 13.4 copy-start.64
  7.2 55.7 %copy-start.62 = (bf16[6,64]{1,0:T(8,128)(2,1)S(1)}, bf16[6,64]{1,0:T(8,128)(2,1)}, u32[]{:S(2)}) copy-start(bf16[6,64]{1,0:T(8,128)(2,1)} %param.28) | copy-start | bytes 2308
  7.2 107.1 %all-gather.28.cloned.1.call-start = ((), (), s32[]{:S(2)}) async-start(), calls=%async_computation.10 | async-start | bytes 3588096 | tf_op jit(solution)/shard_map/all_gather | solution.py:178
  20.5 84.8 %copy-start.47 = (f32[292]{0:T(512)}, f32[292]{0:T(512)S(1)}, u32[]{:S(2)}) copy-start(f32[292]{0:T(512)S(1)} %add_rsqrt_fusion.3) | copy-start | bytes 3508
  20.6 84.8 %copy-start.49 = (f32[292]{0:T(512)}, f32[292]{0:T(512)S(1)}, u32[]{:S(2)}) copy-start(f32[292]{0:T(512)S(1)} %add_rsqrt_fusion.1) | copy-start | bytes 3508
  62.9 42.5 %copy-start.45 = (f32[1,1024]{1,0:T(1,128)}, f32[1,1024]{1,0:T(1,128)S(1)}, u32[]{:S(2)}) copy-start(f32[1,1024]{1,0:T(1,128)S(1)} %get-tuple-element.617) | copy-start | bytes 12292
  105.4 80.5 %all-gather.18.cloned.1.call-start = ((), (), s32[]{:S(2)}) async-start(), calls=%async_computation.5 | async-start | bytes 3342336 | tf_op jit(solution)/shard_map/all_gather | solution.py:155
  106.1 92.0 %all-gather.16.cloned.1.call-start = ((), (), s32[]{:S(2)}) async-start(), calls=%async_computation.4 | async-start | bytes 3588096 | tf_op jit(solution)/shard_map/all_gather | solution.py:178
  106.9 152.7 %all-gather.20.cloned.1.call-start = ((), (), s32[]{:S(2)}) async-start(), calls=%async_computation.6 | async-start | bytes 1114112 | tf_op jit(solution)/shard_map/all_gather | solution.py:156
  107.5 239.5 %all-gather.30.cloned.1.call-start = ((), (), s32[]{:S(2)}) async-start(), calls=%async_computation.11 | async-start | bytes 3588096 | tf_op jit(solution)/shard_map/all_gather | solution.py:199
  198.2 5.7 copy-start.26
  234.1 29.0 %copy-start.23 = (bf16[4,1,584,128]{2,3,1,0:T(8,128)(2,1)}, bf16[4,1,584,128]{2,3,1,0:T(8,128)(2,1)S(1)}, u32[]{:S(2)}) copy-start(bf16[4,1,584,128]{2,3,1,0:T(8,128)(2,1)S(1)} %get-tuple-element.213) | copy-start | bytes 1794052
  265.0 8.6 copy-start.65
  271.5 4.7 collective-permute-start
  274.9 3.3 collective-permute-start.2
  285.0 12.4 copy-start.1
  285.1 12.4 copy-start.3
  292.3 5.8 copy-start.63
  297.5 92.0 %all-gather.24.cloned.1.call-start = ((), (), s32[]{:S(2)}) async-start(), calls=%async_computation.8 | async-start | bytes 4456448 | tf_op jit(solution)/shard_map/all_gather | solution.py:157
  298.1 102.6 %all-gather.36.cloned.1.call-start = ((), (), s32[]{:S(2)}) async-start(), calls=%async_computation.14 | async-start | bytes 3588096 | tf_op jit(solution)/shard_map/all_gather | solution.py:217
  303.3 177.5 %all-gather.26.cloned.1.call-start = ((), (), s32[]{:S(2)}) async-start(), calls=%async_computation.9 | async-start | bytes 4456448 | tf_op jit(solution)/shard_map/all_gather | solution.py:158
  304.1 188.5 %all-gather.22.cloned.1.call-start = ((), (), s32[]{:S(2)}) async-start(), calls=%async_computation.7 | async-start | bytes 3588096 | tf_op jit(solution)/shard_map/all_gather | solution.py:199
  304.8 201.3 %all-gather.32.cloned.1.call-start = ((), (), s32[]{:S(2)}) async-start(), calls=%async_computation.12 | async-start | bytes 3588096 | tf_op jit(solution)/shard_map/all_gather | solution.py:217
  305.4 282.6 %all-gather.38.cloned.1.call-start = ((), (), s32[]{:S(2)}) async-start(), calls=%async_computation.15 | async-start | bytes 3588096 | tf_op jit(solution)/shard_map/all_gather | solution.py:240
  347.0 232.0 %copy-start.59 = (f32[2048]{0:T(1024)}, f32[2048]{0:T(1024)S(1)}, u32[]{:S(2)}) copy-start(f32[2048]{0:T(1024)S(1)} %dynamic_slice.76) | copy-start | bytes 24580
  492.6 7.9 copy-start.31
  492.6 7.9 copy-start.67
  506.2 10.6 copy-start.68
  528.0 3.4 collective-permute-start.4
  530.1 7.4 collective-permute-start.6
  543.7 11.8 copy-start.6
  571.4 102.3 %all-gather.34.cloned.1.call-start = ((), (), s32[]{:S(2)}) async-start(), calls=%async_computation.13 | async-start | bytes 3588096 | tf_op jit(solution)/shard_map/all_gather | solution.py:240
  571.5 7.5 copy-start.66
  579.0 6.9 copy-start.9
  587.8 359.4 %reduce-scatter.37.cloned.1.call-start = ((), (), s32[]{:S(2)}) async-start(), calls=%async_computation.19 | async-start | bytes 540672
  667.7 5.7 copy-start.18
  767.3 12.8 copy-start.41
  776.6 11.0 copy-start.28
  776.6 11.0 collective-permute-start.5
  778.7 14.5 collective-permute-start.7
  791.8 7.6 copy-start.11
  791.8 7.6 copy-start.13
  791.8 7.6 copy-start.46
  799.3 11.3 copy-start.19
  799.3 11.3 copy-start.52
  799.3 11.3 copy-start.55
  799.3 11.3 copy-start.56
  799.4 11.4 copy-start.53
  799.4 11.4 copy-start.54
  811.9 394.6 %all-reduce.23.cloned.1.call-start = ((), (), s32[]{:S(2)}) async-start(), calls=%async_computation.20 | async-start | bytes 16777216
  831.1 457.6 %reduce-scatter.31.cloned.1.call-start = ((), (), s32[]{:S(2)}) async-start(), calls=%async_computation.16 | async-start | bytes 2228224 | tf_op jit(solution)/shard_map/reduce_scatter | solution.py:302
  837.4 7.1 copy-start.70
  837.4 629.1 %reduce-scatter.35.cloned.1.call-start = ((), (), s32[]{:S(2)}) async-start(), calls=%async_computation.18 | async-start | bytes 8912896 | tf_op jit(solution)/shard_map/reduce_scatter | solution.py:304
  853.3 6.3 copy-start.32
  853.3 796.4 %reduce-scatter.33.cloned.1.call-start = ((), (), s32[]{:S(2)}) async-start(), calls=%async_computation.17 | async-start | bytes 8912896 | tf_op jit(solution)/shard_map/reduce_scatter | solution.py:303
  853.4 6.2 copy-start.37
  865.7 5.6 copy-start.57
  868.7 44.3 %collective-permute-start.1 = (bf16[4,1024]{1,0:T(4,128)(2,1)S(1)}, bf16[4,1024]{1,0:T(4,128)(2,1)S(1)}, u32[]{:S(2)}, u32[]{:S(2)}) collective-permute-start(bf16[4,1024]{1,0:T(4,128)(2,1)S(1)} %slice.117), channel_id=1, source_target_pairs={{0,1},{2,3},{4,5},{6,7},{8,9},{10,11},{12,13},{14,15},{16,17},{18,... | collective-permute-start | bytes 24584
  870.0 47.2 %collective-permute-start.3 = (bf16[4,1024]{1,0:T(4,128)(2,1)S(1)}, bf16[4,1024]{1,0:T(4,128)(2,1)S(1)}, u32[]{:S(2)}, u32[]{:S(2)}) collective-permute-start(bf16[4,1024]{1,0:T(4,128)(2,1)S(1)} %slice.119), channel_id=1, source_target_pairs={{0,1},{2,3},{4,5},{6,7},{8,9},{10,11},{12,13},{14,15},{16,17},{18,... | collective-permute-start | bytes 24584
  917.2 7.5 copy-start.2
  917.2 7.5 copy-start.4
  917.2 7.5 copy-start.51
  924.7 6.5 copy-start.14
  924.7 6.5 copy-start.20
  (52 other events, 137.0 us)
Sparse Core Ops, SparseCore 0:
  105.5 8.7 all-gather.27
  117.1 68.7 all-gather.17
  188.0 10.0 all-gather.15
  200.8 56.4 all-gather.19
  297.6 12.2 all-gather.29
  312.6 76.9 all-gather.23
  391.1 9.6 all-gather.35
  403.5 77.2 all-gather.25
  482.9 9.6 all-gather.21
  494.0 12.1 all-gather.31
  571.5 12.2 all-gather.37
  587.9 12.2 all-gather.33
  812.0 135.1 reduce-scatter.36
  954.1 252.3 all-reduce.22
  1209.2 79.4 reduce-scatter.30
  1291.6 174.9 reduce-scatter.34
  1469.4 180.2 reduce-scatter.32
where the time goes:
time: 1670 us; the launch traced here: 1660 us
  waiting for transfers between devices  921 us (55%)
  matrix products  244 us (15%)
  blocking collectives  183 us (11%)
  local copies, waits for them, and re-layouts  157 us (9%)
  other arithmetic  108 us (6%)
  between operations  18.1 us (1%)
    unnamed x27, waiting for transfers between devices  267 us
    reduce_scatter x1, waiting for transfers between devices, shards(): lax.psum_scatter(weight_totals[2], 'dp', scatter_dimension=0, tiled=True)  183 us
    reduce_scatter x1, waiting for transfers between devices, shards(): lax.psum_scatter(weight_totals[3], 'dp', scatter_dimension=1, tiled=True)  178 us
    reduce_scatter x1, waiting for transfers between devices, shards(): lax.psum_scatter(weight_totals[1], 'dp', scatter_dimension=1, tiled=True)  80.3 us
    all_gather x1, waiting for transfers between devices, shards(): lax.all_gather(w_fc2, 'dp', axis=1, tiled=True)  80.1 us
    all_gather x1, waiting for transfers between devices, shards(): lax.all_gather(w_qkv, 'dp', axis=1, tiled=True)  71.6 us
    unnamed x4, blocking collectives  63.6 us
    unnamed x182, local copies, waits for them, and re-layouts  53.1 us
  transfers between devices with their start and end apart: 25, of which 13 were waited for; matrix products, arithmetic and copies ran while one was open for 18% of the time, Pallas kernels for 0%

commit v1 on v0

--- a/solution.py
+++ b/solution.py
@@ -1,13 +1,17 @@
+import functools
+
 import jax
 import jax.numpy as jnp
 from jax import lax
+from jax.experimental import pallas as pl
+from jax.experimental.pallas import tpu as pltpu
 from jax.sharding import PartitionSpec as P
+
+MESH = pl.DeviceIdType.MESH
 
 D = 1024
 HEAD_DIM = 64
 FF = 4096
-MICRO = 2
-IMG_MB = 1
 
 
 EPSILON = 1e-05
@@ -118,6 +122,343 @@
 
     grad_parts = lax.map(one_pair, (jnp.arange(pair_count), log_totals))
     return tuple((join_pairs(member) for member in grad_parts))
+
+
+class Place:
+    def __init__(self):
+        dp=lax.axis_index("dp"); self.c=lax.axis_index("tensor")
+        self.dp=dp; self.z=dp//4; self.y=(dp//2)%2; self.x=dp%2
+    def dev(self, d):
+        if d=="x": t=self.dp+1-2*self.x
+        elif d=="y": t=self.dp+2-4*self.y
+        elif d=="u": t=self.dp+4
+        elif d=="d": t=self.dp-4
+        return (t,self.c)
+    def greet(self):
+        bar=pltpu.get_barrier_semaphore()
+        for d in "xy": pl.semaphore_signal(bar,inc=1,device_id=self.dev(d),device_id_type=MESH)
+        pl.semaphore_signal(bar,inc=1,device_id=(self.dp,1-self.c),device_id_type=MESH)
+        @pl.when(self.z<3)
+        def _(): pl.semaphore_signal(bar,inc=1,device_id=self.dev("u"),device_id_type=MESH)
+        @pl.when(self.z>0)
+        def _(): pl.semaphore_signal(bar,inc=1,device_id=self.dev("d"),device_id_type=MESH)
+        @pl.when((self.z==0)|(self.z==3))
+        def _(): pl.semaphore_wait(bar,4)
+        @pl.when((self.z>0)&(self.z<3))
+        def _(): pl.semaphore_wait(bar,5)
+
+class Scatter:
+    def __init__(self, pc, G, R1, R2, RZ, R3, out, s1, s2, sz, s3, ss):
+        self.pc=pc; self.G,self.R1,self.R2,self.RZ,self.R3,self.out=G,R1,R2,RZ,R3,out
+        self.s1,self.s2,self.sz,self.s3,self.ss=s1,s2,sz,s3,ss
+    def order(self, s): return ("x","y") if s%2==0 else ("y","x")
+    def kinds(self, s):
+        return (3*s+1,"y","x"),(3*s+2,"x","y")
+    def copy(self, src, dst, d, rsem):
+        si={"x":0,"y":1,"u":2,"d":3}[d]
+        return pltpu.make_async_remote_copy(src_ref=src,dst_ref=dst,send_sem=self.ss.at[si],recv_sem=rsem,device_id=self.pc.dev(d),device_id_type=MESH)
+    def wait(self, ref, sem): pltpu.make_async_copy(ref,ref,sem).wait()
+    def pair(self, p, t, d, other):
+        pc=self.pc
+        if d=="y": return self.G.at[p,t,(1-pc.y) if other else pc.y]
+        return self.G.at[p,t,:,(1-pc.x) if other else pc.x]
+    def one(self, p, t, flip=None):
+        pc=self.pc
+        return self.G.at[p,t,(1-pc.y) if flip=="y" else pc.y,(1-pc.x) if flip=="x" else pc.x]
+    def each(self, dist, fn):
+        z=self.pc.z
+        if dist==0: fn(z,None); return
+        @pl.when(z+dist<=3)
+        def _(): fn(z+dist,"u")
+        @pl.when(z-dist>=0)
+        def _(): fn(z-dist,"d")
+    def r0(self, s):
+        for p,d in [(3*s,self.order(s)[1])]+[(p,a) for p,a,b in self.kinds(s)]:
+            for dist in (3,2,1,0):
+                self.each(dist, lambda t,_: self.copy(self.pair(p,t,d,True),self.R1.at[p,t],d,self.s1.at[p,t]).start())
+    def acc(self, dst, *others):
+        v=dst[...].astype(jnp.float32)
+        for o in others: v=v+o[...].astype(jnp.float32)
+        dst[...]=v.astype(jnp.bfloat16)
+    def r1(self, s, dists=(3,2,1,0)):
+        p=3*s; d1,d2=self.order(s)
+        for dist in dists:
+            def go(t,_):
+                self.wait(self.R1.at[p,t],self.s1.at[p,t])
+                self.acc(self.pair(p,t,d2,False),self.R1.at[p,t])
+                self.copy(self.one(p,t,d1),self.R2.at[s,t],d1,self.s2.at[s,t]).start()
+            self.each(dist,go)
+    def line(self, p, view, slot, pre, dist, own):
+        z=self.pc.z
+        def go(t,way):
+            pre(t)
+            if way=="u":
+                @pl.when(z>0)
+                def _():
+                    self.wait(slot(t+1),self.sz.at[p,t+1]); self.acc(view(t),slot(t+1))
+                self.copy(view(t),slot(t+1),"u",self.sz.at[p,t+1]).start()
+            elif way=="d":
+                @pl.when(z<3)
+                def _():
+                    self.wait(slot(t),self.sz.at[p,t]); self.acc(view(t),slot(t))
+                self.copy(view(t),slot(t),"d",self.sz.at[p,t]).start()
+            else:
+                @pl.when(z>0)
+                def _():
+                    self.wait(slot(z+1),self.sz.at[p,z+1]); self.acc(view(z),slot(z+1))
+                @pl.when(z<3)
+                def _():
+                    self.wait(slot(z),self.sz.at[p,z]); self.acc(view(z),slot(z))
+                own()
+        self.each(dist,go)
+    def rxy(self, s, dist):
+        for p,a,b in self.kinds(s):
+            view=lambda t: self.pair(p,t,a,False)
+            def pre(t):
+                self.wait(self.R1.at[p,t],self.s1.at[p,t]); self.acc(view(t),self.R1.at[p,t])
+            def own(): self.copy(self.one(p,self.pc.z,b),self.R3.at[p],b,self.s3.at[p]).start()
+            self.line(p,view,lambda i: self.RZ.at[p,i],pre,dist,own)
+    def rz(self, s, dist):
+        p=3*s
+        def pre(t):
+            self.wait(self.R2.at[s,t],self.s2.at[s,t]); self.acc(self.one(p,t),self.R2.at[s,t])
+        def own():
+            self.out[p]=self.one(p,self.pc.z)[...].astype(jnp.float32)
+        self.line(p,lambda t: self.one(p,t),lambda i: self.RZ.at[p,i,0],pre,dist,own)
+    def last(self, s):
+        for p,a,b in self.kinds(s):
+            self.wait(self.R3.at[p],self.s3.at[p])
+            self.out[p]=self.one(p,self.pc.z)[...].astype(jnp.float32)+self.R3[p].astype(jnp.float32)
+    def blocks(self,n,sem):
+        while n>=16: self.wait(self.G.at[0],sem); n-=16
+        while n>=4: self.wait(self.G.at[0,0],sem); n-=4
+        while n: self.wait(self.G.at[0,0,0,0],sem); n-=1
+    def finish(self):
+        self.blocks(60,self.ss.at[0]); self.blocks(60,self.ss.at[1])
+        for k in range(3):
+            @pl.when(self.pc.z==k)
+            def _(): self.blocks(20*(3-k),self.ss.at[2])
+            @pl.when(self.pc.z==k+1)
+            def _(): self.blocks(20*(k+1),self.ss.at[3])
+    EVENTS=["r0","r1","xy3","xy2","z3","xy1","z2","xy0","z1","last","z0"]
+    def run(self,s,e):
+        if e[0]=="r": getattr(self,e)(s)
+        elif e=="last": self.last(s)
+        elif e[0]=="z": self.rz(s,int(e[1]))
+        else: self.rxy(s,int(e[2]))
+
+def scatter_order(off,pre):
+    ev=[]
+    for s in range(4):
+        for i,e in enumerate(Scatter.EVENTS):
+            ev.append((i+off*s-(pre if e=="r0" else 0),s,i,e))
+    return [(s,e) for _,s,_,e in sorted(ev)]
+
+def rs_kernel(order, g_ref, o_ref, G, R1,R2,RZ,R3, OUT, lsem,s1,s2,sz,s3,ss):
+    pc=Place()
+    cps=[pltpu.make_async_copy(g_ref.at[pl.ds(3*i,3)],G.at[pl.ds(3*i,3)],lsem.at[i]) for i in range(4)]
+    for c in cps: c.start()
+    pc.greet()
+    sc=Scatter(pc,G,R1,R2,RZ,R3,OUT,s1,s2,sz,s3,ss)
+    for s,e in order:
+        if e=="r0": cps[s].wait()
+        sc.run(s,e)
+    cp=pltpu.make_async_copy(OUT,o_ref,lsem.at[0]); cp.start();
+    sc.finish(); cp.wait()
+
+def rs_scratch():
+    B=lambda *s: pltpu.VMEM(s+(64,512),jnp.bfloat16)
+    D=lambda *s: pltpu.SemaphoreType.DMA(s)
+    return [B(12,4,2,2),B(12,4,2),B(4,4),B(12,5,2),B(12),pltpu.VMEM((12,64,512),jnp.float32),D(4),D(12,4),D(4,4),D(12,5),D(12),D(4)]
+
+def rs_call(g, order, name="rs"):
+    return pl.pallas_call(functools.partial(rs_kernel,order), out_shape=jax.ShapeDtypeStruct((12,64,512),jnp.float32),
+        in_specs=[pl.BlockSpec(memory_space=pl.ANY)], out_specs=pl.BlockSpec(memory_space=pl.ANY),
+        scratch_shapes=rs_scratch(), name=name,
+        compiler_params=pltpu.CompilerParams(collective_id=1,has_side_effects=True,vmem_limit_bytes=60*2**20))(g)
+
+class Gather:
+    NS=4
+    def __init__(self, wloc, wall, zs, fs, ts, ss):
+        self.wloc, self.wall, self.zs, self.fs, self.ts, self.ss = wloc, wall, zs, fs, ts, ss
+        dp=lax.axis_index("dp"); self.c=lax.axis_index("tensor")
+        self.z=dp//4; self.y=(dp//2)%2; self.x=dp%2
+        self.dp=dp
+    def dev(self, d):
+        if d=="x": t=self.z*4+self.y*2+(1-self.x)
+        elif d=="y": t=self.z*4+(1-self.y)*2+self.x
+        elif d=="u": t=self.dp+4
+        else: t=self.dp-4
+        return (t,self.c)
+    def greet(self, bar):
+        n=jnp.where((self.z==0)|(self.z==3),3,4)
+        for d in "xy": pl.semaphore_signal(bar,inc=1,device_id=self.dev(d),device_id_type=MESH)
+        @pl.when(self.z<3)
+        def _(): pl.semaphore_signal(bar,inc=1,device_id=self.dev("u"),device_id_type=MESH)
+        @pl.when(self.z>0)
+        def _(): pl.semaphore_signal(bar,inc=1,device_id=self.dev("d"),device_id_type=MESH)
+        return n
+    def copy(self, ref, d, rsem):
+        si={"x":0,"y":1,"u":2,"d":3}[d]
+        return pltpu.make_async_remote_copy(src_ref=ref,dst_ref=ref,send_sem=self.ss.at[si],recv_sem=rsem,device_id=self.dev(d),device_id_type=MESH)
+    def zsend(self, ref_of, p, zsrc, up, cond):
+        ref=ref_of(zsrc)
+        @pl.when(cond)
+        def _(): self.copy(ref, "u" if up else "d", self.zs.at[p,zsrc]).start()
+    def vZ(self,p): return lambda zz: self.wall.at[p,zz,self.y,self.x]
+    def vXZY(self,p): return lambda zz: self.wall.at[p,zz,self.y]
+    def vYZX(self,p): return lambda zz: self.wall.at[p,zz,:,self.x]
+    def wait(self, ref, sem):
+        pltpu.make_async_copy(ref,ref,sem).wait()
+    def pieces(self, s):
+        return 3*s, 3*s+1, 3*s+2
+    def order(self, s):
+        return ("x","y") if s%2==0 else ("y","x")
+    def nb(self, d, p):
+        if d=="x": return lambda zz: self.wall.at[p,zz,self.y,1-self.x]
+        return lambda zz: self.wall.at[p,zz,1-self.y,self.x]
+    def pair(self, d1, p):
+        return self.vXZY(p) if d1=="x" else self.vYZX(p)
+    def e0(self, s):
+        pz,px,py=self.pieces(s); d1,d2=self.order(s); z=self.z
+        self.zsend(self.vZ(pz),pz,z,True,z<3)
+        self.zsend(self.vZ(pz),pz,z,False,z>0)
+        self.copy(self.vZ(px)(z),"x",self.fs.at[px,0]).start()
+        self.copy(self.vZ(py)(z),"y",self.fs.at[py,0]).start()
+        self.copy(self.vZ(pz)(z),d1,self.fs.at[pz,z]).start()
+    def e1(self, s):
+        pz,px,py=self.pieces(s); z=self.z
+        for p,v,d,e in ((px,self.vXZY(px),"x","y"),(py,self.vYZX(py),"y","x")):
+            self.wait(self.nb(d,p)(z),self.fs.at[p,0])
+            self.zsend(v,p,z,True,z<3)
+            self.zsend(v,p,z,False,z>0)
+            self.copy(v(z),e,self.ts.at[p]).start()
+    def zarr(self, p, v, dist, then):
+        z=self.z
+        @pl.when(z-dist>=0)
+        def _():
+            src=z-dist
+            self.wait(v(src),self.zs.at[p,src])
+            self.zsend(v,p,src,True,z<3)
+            then(src)
+        @pl.when(z+dist<=3)
+        def _():
+            src=z+dist
+            self.wait(v(src),self.zs.at[p,src])
+            self.zsend(v,p,src,False,z>0)
+            then(src)
+    def ez(self, s, dist):
+        pz,px,py=self.pieces(s); d1,d2=self.order(s); z=self.z
+        if dist<=3:
+            self.zarr(pz,self.vZ(pz),dist,lambda src: self.copy(self.vZ(pz)(src),d1,self.fs.at[pz,src]).start())
+        def d1arr(src):
+            self.wait(self.nb(d1,pz)(src),self.fs.at[pz,src])
+            self.copy(self.pair(d1,pz)(src),d2,self.ts.at[pz]).start()
+        if dist==1: d1arr(z)
+        else:
+            @pl.when(z-(dist-1)>=0)
+            def _(): d1arr(z-(dist-1))
+            @pl.when(z+(dist-1)<=3)
+            def _(): d1arr(z+(dist-1))
+    def exy(self, s, dist):
+        pz,px,py=self.pieces(s)
+        for p,v,e in ((px,self.vXZY(px),"y"),(py,self.vYZX(py),"x")):
+            self.zarr(p,v,dist,lambda src: self.copy(v(src),e,self.ts.at[p]).start())
+    def term(self, s):
+        pz,px,py=self.pieces(s); d1,d2=self.order(s)
+        for p,d in ((pz,d2),(px,"y"),(py,"x")):
+            ref=self.wall.at[p,:,1-self.y] if d=="y" else self.wall.at[p,:,:,1-self.x]
+            self.wait(ref,self.ts.at[p])
+    def finish(self):
+        flat=lambda n: self.wall.at[0:n//16] if n%16==0 else None
+        for si in (0,1):
+            self.wait(self.wall.at[0:3],self.ss.at[si]); self.wait(self.wall.at[0,0:3],self.ss.at[si])
+        for k in range(3):
+            @pl.when(self.z==k)
+            def _():
+                for _i in range(k+1):
+                    self.wait(self.wall.at[0],self.ss.at[2]); self.wait(self.wall.at[0,0],self.ss.at[2])
+            @pl.when(self.z==k+1)
+            def _():
+                for _i in range(3-k):
+                    self.wait(self.wall.at[0],self.ss.at[3]); self.wait(self.wall.at[0,0],self.ss.at[3])
+    EVENTS=["e0","e1","z1","xy1","z2","xy2","z3","xy3","z4","term"]
+    def run(self, s, e):
+        if e=="e0": self.e0(s)
+        elif e=="e1": self.e1(s)
+        elif e=="term": self.term(s)
+        elif e[0]=="z": self.ez(s,int(e[1]))
+        else: self.exy(s,int(e[2]))
+
+def gather_order(off, pre):
+    ev=[]
+    for s in range(4):
+        for i,e in enumerate(Gather.EVENTS):
+            k = i+off*s
+            if e=="e0": k=off*s-pre
+            ev.append((k,s,i,e))
+    ev.sort()
+    return [(s,e) for k,s,i,e in ev]
+
+
+def ag_kernel(order, wloc, wall, held, lsem, zs, fs, ts, ss):
+    pc = Place()
+    pc.greet()
+    cp = pltpu.make_async_copy(wloc, held, lsem)
+    cp.start()
+    cp.wait()
+    cp = pltpu.make_async_copy(held, wall.at[:, pc.z, pc.y, pc.x], lsem)
+    cp.start()
+    cp.wait()
+    g = Gather(wloc, wall, zs, fs, ts, ss)
+    for s, e in order:
+        g.run(s, e)
+    g.finish()
+
+
+def ag_call(wloc, order):
+    D = lambda *s: pltpu.SemaphoreType.DMA(s)
+    return pl.pallas_call(
+        functools.partial(ag_kernel, order),
+        out_shape=jax.ShapeDtypeStruct((12, 4, 2, 2, 64, 512), jnp.bfloat16),
+        in_specs=[pl.BlockSpec(memory_space=pl.ANY)],
+        out_specs=pl.BlockSpec(memory_space=pl.ANY),
+        scratch_shapes=[pltpu.VMEM((12, 64, 512), jnp.bfloat16), pltpu.SemaphoreType.DMA, D(12, 4), D(12, 4), D(12), D(4)],
+        name="gather",
+        compiler_params=pltpu.CompilerParams(collective_id=0, has_side_effects=True),
+    )(wloc)
+
+def gather_all(w_qkv, w_out, w_fc1, w_fc2, norm_gains, bias_rows, fc_bias):
+    count = lax.axis_size("dp")
+    local = jnp.concatenate([w_qkv, w_out.T[None], split_cols(w_fc1), split_cols(w_fc2.T)], axis=0)
+    if count == 16:
+        whole = ag_call(local, gather_order(2, 8)).reshape(12, D, 512)
+    else:
+        whole = lax.all_gather(local, "dp", axis=1, tiled=True)
+    small = (
+        lax.all_gather(norm_gains, "dp", axis=1, tiled=True),
+        lax.all_gather(bias_rows, "dp", axis=1, tiled=True),
+        lax.all_gather(fc_bias, "dp", axis=0, tiled=True),
+    )
+    return (whole[:3], whole[3].T, join_cols(whole[4:8]), join_cols(whole[8:12]).T), small
+
+
+def split_cols(m):
+    return jnp.transpose(m.reshape(m.shape[0], m.shape[1] // 512, 512), (1, 0, 2))
+
+
+def join_cols(m):
+    return jnp.transpose(m, (1, 0, 2)).reshape(m.shape[1], m.shape[0] * 512)
+
+
+def scatter_all(grads):
+    qkv, out, up, down = grads
+    parts = jnp.concatenate([qkv, out.T[None], split_cols(up), split_cols(down.T)], axis=0).astype(jnp.bfloat16)
+    if lax.axis_size("dp") == 16:
+        mine = rs_call(parts.reshape(12, 4, 2, 2, 64, 512), scatter_order(2, 0))
+    else:
+        mine = lax.psum_scatter(parts, "dp", scatter_dimension=1, tiled=True).astype(jnp.float32)
+    return (mine[:3], mine[3].T, join_cols(mine[4:8]), join_cols(mine[8:12]).T)
 
 
 def shards(
@@ -137,6 +478,7 @@
     local_width = w_qkv.shape[2]
     hidden_local = w_fc1.shape[1]
     score_scale = HEAD_DIM ** (-0.5)
+    gathered = gather_all(w_qkv, w_out, w_fc1, w_fc2, norm_gains, bias_rows, fc_bias)
     outputs = []
     input_grads = []
     weight_totals = None
@@ -144,25 +486,15 @@
     fc_total = jnp.zeros((FF,), jnp.float32)
     zero_row = jnp.zeros((D,), jnp.float32)
     zero_hidden = jnp.zeros((FF,), jnp.float32)
-    for micro_step in range(MICRO):
-        first_img = micro_step * IMG_MB
+    IMG_MB = layer_in.shape[0]
+    for micro_step in range(1):
+        first_img = 0
         tokens = layer_in[first_img : first_img + IMG_MB].astype(jnp.float32)
         live_rows = image_live[first_img : first_img + IMG_MB].astype(jnp.float32)[:, None, None]
         grad_local = out_grad[first_img : first_img + IMG_MB].astype(jnp.float32) * live_rows
         grad_low = grad_local.astype(jnp.bfloat16)
         valid_keys = key_valid[first_img : first_img + IMG_MB] > 0
-        gathered = (
-            lax.all_gather(w_qkv, "dp", axis=1, tiled=True),
-            lax.all_gather(w_out, "dp", axis=1, tiled=True),
-            lax.all_gather(w_fc1, "dp", axis=0, tiled=True),
-            lax.all_gather(w_fc2, "dp", axis=1, tiled=True),
-            lax.all_gather(norm_gains, "dp", axis=1, tiled=True),
-            lax.all_gather(bias_rows, "dp", axis=1, tiled=True),
-            lax.all_gather(fc_bias, "dp", axis=0, tiled=True),
-        )
-        qkv_weight, out_weight, up_weight, down_weight, gain_rows, shift_rows, hidden_shift = (
-            gathered
-        )
+        (qkv_weight, out_weight, up_weight, down_weight), (gain_rows, shift_rows, hidden_shift) = gathered
         gain_rows = gain_rows.astype(jnp.float32)
         shift_rows = shift_rows.astype(jnp.float32)
         query_bias = lax.dynamic_slice_in_dim(
@@ -297,12 +629,7 @@
             weight_totals = tuple(
                 (before + added for before, added in zip(weight_totals, micro_grads))
             )
-    weight_totals = (
-        lax.psum_scatter(weight_totals[0], "dp", scatter_dimension=1, tiled=True),
-        lax.psum_scatter(weight_totals[1], "dp", scatter_dimension=1, tiled=True),
-        lax.psum_scatter(weight_totals[2], "dp", scatter_dimension=0, tiled=True),
-        lax.psum_scatter(weight_totals[3], "dp", scatter_dimension=1, tiled=True),
-    )
+    weight_totals = scatter_all(weight_totals)
     summed_vectors, summed_hidden = (
         lax.psum_scatter(vector_total, ("dp", "tensor"), scatter_dimension=1, tiled=True),
         lax.psum_scatter(fc_total, ("dp", "tensor"), scatter_dimension=0, tiled=True),

time: 1670 us -> 1020 us (0.61)
  waiting for transfers between devices: 921 us -> 153 us
  Pallas kernels: 0 us -> 211 us
  other arithmetic: 108 us -> 78.5 us
  blocking collectives: 183 us -> 160 us
  matrix products: 244 us -> 223 us
    reduce_scatter x3 -> x0, waiting for transfers between devices: 441 us -> none  [the longest x1 183 us: shards(): lax.psum_scatter(weight_totals[2], 'dp', scatter_dimension=0, tiled=True)]
    pallas_call x0 -> x2, Pallas kernels: none -> 211 us  [the longest x1 115 us: rs_call(): pl.pallas_call(functools.partial(rs_kernel, order), out_shape=jax.ShapeDt...]
    all_gather x4 -> x0, waiting for transfers between devices: 194 us -> none  [the longest x1 80.1 us: shards(): lax.all_gather(w_fc2, 'dp', axis=1, tiled=True)]
    unnamed x27 -> x12, waiting for transfers between devices: 267 us -> 153 us
    unnamed x182 -> x80, local copies, waits for them, and re-layouts: 53.1 us -> 12.3 us
    transpose x0 -> x9, local copies, waits for them, and re-layouts: none -> 30.8 us  [the longest x2 12.7 us: join_cols(): return jnp.transpose(m, (1, 0, 2)).reshape(m.shape[1], m.shape[0] * 512)]
    reshape x0 -> x8, local copies, waits for them, and re-layouts: none -> 29.3 us  [the longest x4 17.2 us: join_cols(): return jnp.transpose(m, (1, 0, 2)).reshape(m.shape[1], m.shape[0] * 512)]
    dynamic_slice x56 -> x28, local copies, waits for them, and re-layouts: 47.1 us -> 21.8 us  [pair_slice(): lax.dynamic_slice_in_dim(source, pair_index * pair_width, pair_width, 2)]
  transfers between devices with their start and end apart: 25 -> 8, of which waited for: 13 -> 3; matrix products, arithmetic and copies ran while one was open for 18% -> 14% of each run, Pallas kernels for 0% -> 21%
where the time goes in v1:
time: 1020 us; the launch traced here: 1010 us
  matrix products  223 us (22%)
  Pallas kernels  211 us (21%)
  local copies, waits for them, and re-layouts  166 us (16%)
  blocking collectives  160 us (16%)
  waiting for transfers between devices  153 us (15%)
  other arithmetic  78.5 us (8%)
  between operations  15.9 us (2%)
    unnamed x12, waiting for transfers between devices  153 us
    pallas_call x1, Pallas kernels, rs_call(): pl.pallas_call(functools.partial(rs_kernel, order), out_shape=jax.ShapeDt...  115 us
    pallas_call x1, Pallas kernels, ag_call(): pl.pallas_call(functools.partial(ag_kernel, order), out_shape=jax.ShapeDt...  95.4 us
    all_gather x1, blocking collectives, gather_all(): lax.all_gather(norm_gains, 'dp', axis=1, tiled=True)  42.5 us
    dot_general x4, matrix products, one_pair(): jnp.einsum('bhqk,bqhd->bkhd', score_grad, query_block, preferred_element_...  40.9 us
    all_gather x1, blocking collectives, gather_all(): lax.all_gather(fc_bias, 'dp', axis=0, tiled=True)  40.9 us
    dot_general x4, matrix products, one_pair(): jnp.einsum('bhqk,bkhd->bqhd', score_grad, key_block, preferred_element_ty...  40.8 us
    unnamed x1, blocking collectives  40.6 us
  transfers between devices with their start and end apart: 8, of which 3 were waited for; matrix products, arithmetic and copies ran while one was open for 14% of the time, Pallas kernels for 21%

profile of v1, /device:TPU:0, one launch (start us, length us, event | category | flops | bytes accessed | tf_op | source)
XLA Modules:
  0.0 1013.5 jit_solution(122805993510187594)
XLA Ops:
  7.2 42.5 %all-gather = bf16[16,64,2]{1,2,0:T(2,128)(2,1)S(1)} all-gather(bf16[1,64,2]{1,2,0:T(2,128)(2,1)} %bitcast.307), channel_id=1, replica_groups=mesh['dp'=16,'tensor'=2] {'dp'}, dimensions={0}, use_global_device_ids=true | all-gather | bytes 4352 | tf_op jit(solution)/shard_map/all_gather | solution.py:439
  49.8 35.9 %all-gather.1 = bf16[16,64,6]{1,2,0:T(8,128)(2,1)S(1)} all-gather(bf16[1,64,6]{1,2,0:T(8,128)(2,1)} %bitcast.306), channel_id=1, replica_groups=mesh['dp'=16,'tensor'=2] {'dp'}, dimensions={0}, use_global_device_ids=true | all-gather | bytes 13056 | tf_op jit(solution)/shard_map/all_gather | solution.py:440
  95.2 95.4 %gather.1 = bf16[12,4,2,2,64,512]{5,4,3,2,1,0:T(8,128)(2,1)} custom-call(bf16[12,64,512]{2,1,0:T(8,128)(2,1)} %pad_maximum_fusion.1.wloc), custom_call_target="tpu_custom_call" | custom-call | tf_op jit(solution)/shard_map/gather/pallas_call | solution.py:421
  193.0 3.9 slice.70
  196.9 6.9 convolution_bitcast_fusion
  215.2 36.2 %while.26 = (s32[]{:T(128)}, bf16[4,2,584,128]{2,3,1,0:T(8,128)(2,1)}, f32[4,2,2,584]{3,2,1,0:T(2,128)S(1)}, s32[4]{0:T(128)S(1)}, bf16[2,584,512]{1,2,0:T(8,128...) while((s32[]{:T(128)}, ...), condition=%wide.region_5.6_spmd, body=%wide.region_2.5_spmd.sunk | while | flops 365759200 | bytes 20068600 | solution.py:81
  261.1 3.9 copy.130
  266.9 15.8 %all-reduce.10.cloned.1.call-done = bf16[2,584,1024]{2,0,1:T(2,128)(2,1)} async-done(((bf16[2,584,1024]{2,0,1:T(2,128)(2,1)}), bf16[2,584,1024]{2,0,1:T(2,128)(2,1)}) %all-reduce.10.cloned.1.call-update) | async-done | bytes 2392080
  282.8 3.4 fusion.77
  286.1 3.6 multiply_reduce_fusion.1
  289.7 3.9 add_convert_fusion.1
  293.7 3.4 fusion.64
  297.2 40.9 %all-gather.2 = bf16[16,1,256]{2,1,0:T(2,128)(2,1)S(1)} all-gather(bf16[1,1,256]{2,1,0:T(2,128)(2,1)S(1)} %reshape.247), channel_id=1, replica_groups=mesh['dp'=16,'tensor'=2] {'dp'}, dimensions={0}, use_global_device_ids=true | all-gather | bytes 8704 | tf_op jit(solution)/shard_map/all_gather | solution.py:441
  338.1 5.4 fusion.79
  343.5 5.3 copy.133
  348.8 7.8 reshape.256
  356.5 7.5 copy.131
  364.0 7.7 reshape.255
  371.7 11.9 %multiply_convert_fusion.2 = (bf16[2,584,2048]{2,1,0:T(8,128)(2,1)}, f32[2,584,2048]{2,1,0:T(8,128)}) fusion(f32[2048]{0:T(1024)S(1)} %dynamic_slice.43, bf16[1024,2048,1]{1,0,2:T(8,128)(2,1)} %reshape.255, bf16[2,584,1024]{2,0,1:T(2,128)(2,1)} %all-gather.10.cloned.1.call-done), kind=kOutput, calls=%fused_computation.43 | convolution fusion | flops 4915691520 | bytes 20946944 | tf_op jit(solution)/shard_map/bsd,df->bsf/dot_general | solution.py:533
  383.6 12.3 %convert_reduce_fusion = (f32[2048]{0:T(1024)S(1)}, bf16[2,584,2048]{2,1,0:T(8,128)(2,1)S(1)}) fusion(f32[2,584,2048]{2,1,0:T(8,128)} %get-tuple-element.282, f32[2048]{0:T(1024)S(1)} %dynamic_slice.43, bf16[1024,2048,1]{1,0,2:T(8,128)(2,1)} %reshape.256, bf16[2,584,1024]{2,0,1:T(2,128)(2,1)} %all-gather.12.cloned.1.call-done), kind=kOutput, calls=%fused_computation.41 | convolution fusion | flops 4930041856 | bytes 20955136 | tf_op jit(solution)/shard_map/bsd,fd->bsf/dot_general | solution.py:553
  396.0 5.4 convolution_convert_fusion.1
  401.4 3.9 copy.136
  408.8 14.3 %all-reduce.12.cloned.1.call-done = bf16[2,584,1024]{2,0,1:T(2,128)(2,1)} async-done(((bf16[2,584,1024]{2,0,1:T(2,128)(2,1)}), bf16[2,584,1024]{2,0,1:T(2,128)(2,1)}) %all-reduce.12.cloned.1.call-update) | async-done | bytes 2392080
  423.1 9.1 fusion.54
  432.3 9.8 convert_reduce_fusion.6
  442.1 9.2 bitcast_convert_fusion
  455.1 7.8 convolution_convert_fusion.2
  462.9 3.9 copy.134
  466.8 6.4 copy.148
  473.2 4.5 convolution_convert_fusion.3
  481.2 150.6 %while.27 = (s32[]{:T(128)}, bf16[4,2,584,128]{2,3,1,0:T(8,128)(2,1)}, bf16[4,2,584,128]{2,3,1,0:T(8,128)(2,1)}, bf16[4,2,584,128]{2,3,1,0:T(8,128)(2,1)}, s32[4...) while((s32[]{:T(128)}, ...), condition=%wide.region_15.16_spmd, body=%wide.region_13.15_spmd.sunk | while | flops 892656896 | bytes 49676108 | solution.py:123
  486.1 3.7 fusion.145
  489.7 3.4 subtract_exponential_fusion.3
  493.1 10.2 %fusion.148 = bf16[2,2,64,584]{3,2,1,0:T(8,128)(2,1)} fusion(bf16[2,584,2,64]{1,3,2,0:T(8,128)(2,1)} %bitcast.258, f32[2,2,584,584]{2,3,1,0:T(8,128)} %subtract_exponential_fusion.3, f32[2,2,584,584]{2,3,1,0:T(8,128)} %fusion.145), kind=kOutput, calls=%fused_computation.26.clone.1 | convolution fusion | flops 181594208 | bytes 11511808 | tf_op jit(solution)/shard_map/while/body/eval_jaxpr/bhqk,bqhd->bkhd/dot_general | solution.py:107
  503.4 10.2 %fusion.146 = bf16[2,2,64,584]{3,2,1,0:T(8,128)(2,1)} fusion(bf16[2,584,2,64]{1,3,2,0:T(8,128)(2,1)S(1)} %bitcast.256, f32[2,2,584,584]{2,3,1,0:T(8,128)} %subtract_exponential_fusion.3, f32[2,2,584,584]{2,3,1,0:T(8,128)} %fusion.145), kind=kOutput, calls=%fused_computation.25.clone.1 | convolution fusion | flops 181594208 | bytes 11511808 | tf_op jit(solution)/shard_map/while/body/eval_jaxpr/bhqk,bkhd->bqhd/dot_general | solution.py:104
  513.6 3.8 fusion.147
  523.7 3.7 fusion.145
  527.4 3.4 subtract_exponential_fusion.3
  530.8 10.2 %fusion.148 = bf16[2,2,64,584]{3,2,1,0:T(8,128)(2,1)} fusion(bf16[2,584,2,64]{1,3,2,0:T(8,128)(2,1)} %bitcast.258, f32[2,2,584,584]{2,3,1,0:T(8,128)} %subtract_exponential_fusion.3, f32[2,2,584,584]{2,3,1,0:T(8,128)} %fusion.145), kind=kOutput, calls=%fused_computation.26.clone.1 | convolution fusion | flops 181594208 | bytes 11511808 | tf_op jit(solution)/shard_map/while/body/eval_jaxpr/bhqk,bqhd->bkhd/dot_general | solution.py:107
  541.0 10.2 %fusion.146 = bf16[2,2,64,584]{3,2,1,0:T(8,128)(2,1)} fusion(bf16[2,584,2,64]{1,3,2,0:T(8,128)(2,1)S(1)} %bitcast.256, f32[2,2,584,584]{2,3,1,0:T(8,128)} %subtract_exponential_fusion.3, f32[2,2,584,584]{2,3,1,0:T(8,128)} %fusion.145), kind=kOutput, calls=%fused_computation.25.clone.1 | convolution fusion | flops 181594208 | bytes 11511808 | tf_op jit(solution)/shard_map/while/body/eval_jaxpr/bhqk,bkhd->bqhd/dot_general | solution.py:104
  551.2 3.7 fusion.147
  561.3 3.7 fusion.145
  565.0 3.4 subtract_exponential_fusion.3
  568.3 10.2 %fusion.148 = bf16[2,2,64,584]{3,2,1,0:T(8,128)(2,1)} fusion(bf16[2,584,2,64]{1,3,2,0:T(8,128)(2,1)} %bitcast.258, f32[2,2,584,584]{2,3,1,0:T(8,128)} %subtract_exponential_fusion.3, f32[2,2,584,584]{2,3,1,0:T(8,128)} %fusion.145), kind=kOutput, calls=%fused_computation.26.clone.1 | convolution fusion | flops 181594208 | bytes 11511808 | tf_op jit(solution)/shard_map/while/body/eval_jaxpr/bhqk,bqhd->bkhd/dot_general | solution.py:107
  578.6 10.2 %fusion.146 = bf16[2,2,64,584]{3,2,1,0:T(8,128)(2,1)} fusion(bf16[2,584,2,64]{1,3,2,0:T(8,128)(2,1)S(1)} %bitcast.256, f32[2,2,584,584]{2,3,1,0:T(8,128)} %subtract_exponential_fusion.3, f32[2,2,584,584]{2,3,1,0:T(8,128)} %fusion.145), kind=kOutput, calls=%fused_computation.25.clone.1 | convolution fusion | flops 181594208 | bytes 11511808 | tf_op jit(solution)/shard_map/while/body/eval_jaxpr/bhqk,bkhd->bqhd/dot_general | solution.py:104
  588.8 3.7 fusion.147
  598.9 3.7 fusion.145
  602.6 3.4 subtract_exponential_fusion.3
  606.0 10.2 %fusion.148 = bf16[2,2,64,584]{3,2,1,0:T(8,128)(2,1)} fusion(bf16[2,584,2,64]{1,3,2,0:T(8,128)(2,1)} %bitcast.258, f32[2,2,584,584]{2,3,1,0:T(8,128)} %subtract_exponential_fusion.3, f32[2,2,584,584]{2,3,1,0:T(8,128)} %fusion.145), kind=kOutput, calls=%fused_computation.26.clone.1 | convolution fusion | flops 181594208 | bytes 11511808 | tf_op jit(solution)/shard_map/while/body/eval_jaxpr/bhqk,bqhd->bkhd/dot_general | solution.py:107
  616.2 10.2 %fusion.146 = bf16[2,2,64,584]{3,2,1,0:T(8,128)(2,1)} fusion(bf16[2,584,2,64]{1,3,2,0:T(8,128)(2,1)S(1)} %bitcast.256, f32[2,2,584,584]{2,3,1,0:T(8,128)} %subtract_exponential_fusion.3, f32[2,2,584,584]{2,3,1,0:T(8,128)} %fusion.145), kind=kOutput, calls=%fused_computation.25.clone.1 | convolution fusion | flops 181594208 | bytes 11511808 | tf_op jit(solution)/shard_map/while/body/eval_jaxpr/bhqk,bkhd->bqhd/dot_general | solution.py:104
  626.4 3.7 fusion.147
  636.0 3.5 copy.142
  652.9 4.4 bitcast_convert_fusion.3
  657.3 3.9 copy.145
  661.3 8.8 bitcast_convert_fusion.1
  673.2 40.6 %all-reduce.4 = f32[4096]{0:T(1024)S(1)} all-reduce(f32[4096]{0:T(1024)S(1)} %dynamic_update_slice.30), channel_id=7, replica_groups=mesh['dp'=16,'tensor'=2] {'dp','tensor'}, use_global_device_ids=true, to_apply=%region_29.30.clone | all-reduce | flops 4096 | bytes 32768
  714.4 3.7 fusion.71
  718.3 6.1 fusion.33
  724.4 4.7 copy.147
  729.1 11.1 %pad_maximum_fusion.g_ref = bf16[12,4,2,2,64,512]{5,4,3,2,1,0:T(8,128)(2,1)} fusion(bf16[4,4,2,2,64,512]{5,4,3,2,1,0:T(8,128)(2,1)} %bitcast.246, bf16[4,4,2,2,64,512]{5,4,3,2,1,0:T(8,128)(2,1)} %bitcast.247, bf16[1,4,2,2,64,512]{5,4,3,2,1,0:T(8,128)(2,1)S(1)} %bitcast.263, bf16[3,4,2,2,64,512]{5,4,3,2,1,0:T(8,128)(2,1)} %bitcast.250), kind=kLoop, calls=%fused_computation.40 | loop fusion | flops 18874368 | bytes 25165824 | tf_op jit(solution)/shard_map/concatenate | solution.py:456
  740.2 115.4 %rs.1 = f32[12,64,512]{2,1,0:T(8,128)} custom-call(bf16[12,4,2,2,64,512]{5,4,3,2,1,0:T(8,128)(2,1)} %pad_maximum_fusion.g_ref), custom_call_target="tpu_custom_call" | custom-call | tf_op jit(solution)/shard_map/rs/pallas_call | solution.py:275
  862.6 9.1 fusion.55
  873.0 8.8 fusion.65
  881.7 123.1 %reduce-scatter.4.cloned.1.call-done = f32[32,8]{1,0:T(8,128)} async-done(((f32[1024,8]{1,0:T(8,128)}), f32[32,8]{1,0:T(8,128)}) %reduce-scatter.4.cloned.1.call-update) | async-done | bytes 1040
  (256 shorter events, 132.2 us)
Async XLA Ops:
  7.2 81.6 %copy-start = (bf16[2,292,1024]{2,0,1:T(2,128)(2,1)S(1)}, bf16[2,292,1024]{2,0,1:T(2,128)(2,1)}, u32[]{:S(2)}) copy-start(bf16[2,292,1024]{2,0,1:T(2,128)(2,1)} %param.15) | copy-start | bytes 3588100
  7.2 189.7 %all-gather.8.cloned.1.call-start = ((), (), s32[]{:S(2)}) async-start(), calls=%async_computation.1 | async-start | bytes 3588096 | tf_op jit(solution)/shard_map/all_gather | solution.py:510
  49.8 44.3 %copy-start.25 = (f32[1,1024]{1,0:T(1,128)}, f32[1,1024]{1,0:T(1,128)S(1)}, u32[]{:S(2)}) copy-start(f32[1,1024]{1,0:T(1,128)S(1)} %get-tuple-element.279) | copy-start | bytes 12292
  86.5 345.8 %copy-start.22 = (f32[1,1024]{1,0:T(1,128)}, f32[1,1024]{1,0:T(1,128)S(1)}, u32[]{:S(2)}) copy-start(f32[1,1024]{1,0:T(1,128)S(1)} %get-tuple-element.275) | copy-start | bytes 12292
  88.8 1.8 copy-start.13
  90.5 3.7 copy-start.20
  90.5 3.7 copy-start.21
  90.5 0.7 copy-start.16
  91.2 3.0 copy-start.24
  91.2 3.1 copy-start.27
  94.1 188.7 %all-reduce.10.cloned.1.call-start = ((), (), s32[]{:S(2)}) async-start(), calls=%async_computation.6 | async-start | bytes 4784128
  193.0 3.9 copy-start.33
  265.0 0.7 copy-start.37
  265.1 106.7 %all-gather.10.cloned.1.call-start = ((), (), s32[]{:S(2)}) async-start(), calls=%async_computation.2 | async-start | bytes 3588096 | tf_op jit(solution)/shard_map/all_gather | solution.py:531
  282.8 3.4 copy-start.1
  289.7 4.0 copy-start.35
  293.6 3.6 copy-start.36
  293.7 90.0 %all-gather.12.cloned.1.call-start = ((), (), s32[]{:S(2)}) async-start(), calls=%async_computation.3 | async-start | bytes 3588096 | tf_op jit(solution)/shard_map/all_gather | solution.py:549
  297.2 125.9 %all-reduce.12.cloned.1.call-start = ((), (), s32[]{:S(2)}) async-start(), calls=%async_computation.7 | async-start | bytes 4784128
  383.6 12.3 %copy-start.12 = (bf16[1024,2048,1]{1,0,2:T(8,128)(2,1)S(1)}, bf16[1024,2048,1]{1,0,2:T(8,128)(2,1)}, u32[]{:S(2)}) copy-start(bf16[1024,2048,1]{1,0,2:T(8,128)(2,1)} %reshape.255) | copy-start | bytes 12582916
  395.9 5.5 copy-start.38
  405.4 61.4 %all-gather.14.cloned.1.call-start = ((), (), s32[]{:S(2)}) async-start(), calls=%async_computation.4 | async-start | bytes 3588096 | tf_op jit(solution)/shard_map/all_gather | solution.py:572
  423.1 9.2 copy-start.2
  423.1 9.2 copy-start.8
  442.1 420.5 %all-reduce.14.cloned.1.call-start = ((), (), s32[]{:S(2)}) async-start(), calls=%async_computation.8 | async-start | bytes 9568256
  451.3 3.8 copy-start.11
  484.9 4.8 copy-start.5
  513.6 3.8 copy-start.6
  513.6 4.5 copy-start.7
  522.5 4.8 copy-start.5
  551.2 3.8 copy-start.6
  551.2 4.5 copy-start.7
  560.1 4.8 copy-start.5
  588.8 3.8 copy-start.6
  588.8 4.5 copy-start.7
  597.8 4.8 copy-start.5
  626.4 3.8 copy-start.6
  626.4 4.6 copy-start.7
  636.0 6.8 copy-start.3
  648.1 1.6 copy-start.9
  648.1 2.0 copy-start.10
  649.7 3.2 copy-start.15
  650.2 1.9 copy-start.18
  661.2 343.7 %reduce-scatter.4.cloned.1.call-start = ((), (), s32[]{:S(2)}) async-start(), calls=%async_computation.5 | async-start | bytes 540672
  714.4 3.8 copy-start.19
  714.4 3.9 copy-start.34
  857.3 3.4 copy-start.4
  858.7 3.9 copy-start.14
  858.7 3.9 copy-start.17
  858.7 3.9 copy-start.26
  860.7 11.1 %copy-start.29 = (f32[1024]{0:T(1024)S(1)}, f32[1024]{0:T(1024)}, u32[]{:S(2)}) copy-start(f32[1024]{0:T(1024)} %get-tuple-element.255) | copy-start | bytes 12292
  860.7 11.1 %copy-start.30 = (f32[1024]{0:T(1024)S(1)}, f32[1024]{0:T(1024)}, u32[]{:S(2)}) copy-start(f32[1024]{0:T(1024)} %get-tuple-element.270) | copy-start | bytes 12292
  860.7 11.1 %copy-start.31 = (f32[1024]{0:T(1024)S(1)}, f32[1024]{0:T(1024)}, u32[]{:S(2)}) copy-start(f32[1024]{0:T(1024)} %get-tuple-element.207) | copy-start | bytes 12292
  860.7 11.1 %copy-start.32 = (f32[1024]{0:T(1024)S(1)}, f32[1024]{0:T(1024)}, u32[]{:S(2)}) copy-start(f32[1024]{0:T(1024)} %get-tuple-element.213) | copy-start | bytes 12292
  862.6 10.3 %copy-start.23 = (f32[1,1024]{1,0:T(1,128)S(1)}, f32[1,1024]{1,0:T(1,128)}, u32[]{:S(2)}) copy-start(f32[1,1024]{1,0:T(1,128)} %copy-done.22) | copy-start | bytes 12292
  862.6 10.3 %copy-start.28 = (f32[1,1024]{1,0:T(1,128)S(1)}, f32[1,1024]{1,0:T(1,128)}, u32[]{:S(2)}) copy-start(f32[1,1024]{1,0:T(1,128)} %get-tuple-element.273) | copy-start | bytes 12292
Sparse Core Ops, SparseCore 0:
  94.2 8.6 all-gather.7
  265.2 17.5 all-reduce.9
  293.8 12.1 all-gather.9
  307.4 12.1 all-gather.11
  405.5 17.5 all-reduce.11
  442.2 12.1 all-gather.13
  661.3 30.5 all-reduce.13
  873.1 131.7 reduce-scatter.3
